TPU v7x, 32 devices: a whole 2x2x4 slice. The times are simulated.
32 devices in a mesh: dp: 8 (over z, x), context: 4 (over y, core).
Axes of the slice: x: 2, y: 2, z: 4, core: 2. Of those that a mesh axis runs over, the one named last changes fastest.
Arguments:
- values: bfloat16 [1024, 4096], P('context', 'dp'), may hold values from -6 to 6
- gates: bfloat16 [1024, 4096], P('context', 'dp'), may hold values from -6 to 6
- filters: float32 [1024, 512], P('context'), may hold values from -6 to 6
- skips: float32 [4096], P('dp'), may hold values from 0.5 to 1.5
- grad_out: bfloat16 [1024, 4096], P('context', 'dp'), may hold values from -6 to 6
Outputs:
- mixed: bfloat16 [1024, 4096], P('context', 'dp')
- grad_gates: bfloat16 [1024, 4096], P('context', 'dp')
- grad_values: bfloat16 [1024, 4096], P('context', 'dp')
- grad_filters: float32 [1024, 512], P('context')
All inputs are finite; a program needn't handle non-finite values.
Results may differ from a plain program's by a relative error of at most 0.001.
Values may be sent and summed in bfloat16 or wider, within the bound.
A program may use at most 128 MiB of HBM per device.

v0:
```python
from functools import partial
import math

import jax
import jax.numpy as jnp
import numpy as np
from jax import lax
from jax.experimental import pallas as pl
from jax.experimental.pallas import tpu as pltpu
from jax.sharding import PartitionSpec as P

LANES = 128
STRIP = 16


def plan(length):
    inner = 128
    while 2 * length // inner > 32:
        inner *= 2
    return 2 * length // inner, inner


def tables(length):
    outer, inner = plan(length)
    total = 2 * length
    pos = np.arange(inner, dtype=np.int64)[None, :]
    freq = np.arange(inner, dtype=np.int64)[:, None]
    fwd, inv = [], []
    for k in range(outer // 2 + 1):
        angle = -2.0 * np.pi / total * ((pos * (k + outer * freq)) % total)
        c, s = np.cos(angle), np.sin(angle)
        m = np.block([[c, -s], [s, c]])
        fwd.append(m)
        weight = (1.0 if k in (0, outer // 2) else 1.0) / total / math.sqrt(length)
        inv.append(m.T * weight)

    def split(stack):
        full = np.stack(stack).astype(np.float32)
        hi = full.astype(jnp.bfloat16)
        lo = (full - hi.astype(np.float32)).astype(jnp.bfloat16)
        return hi, lo

    return split(fwd) + split(inv)


def add(a, b):
    if a is None:
        return b
    return a if b is None else a + b


def sub(a, b):
    if b is None:
        return a
    return -b if a is None else a - b


def rotate(z, turn):
    re, im = z
    eighth = round(turn * 8) % 8 if abs(turn * 8 - round(turn * 8)) < 1e-9 else None
    if eighth == 0:
        return z
    if eighth == 4:
        return sub(None, re) if re is not None else None, sub(None, im) if im is not None else None
    if eighth == 2:
        return (None if im is None else -im), re
    if eighth == 6:
        return im, (None if re is None else -re)
    c, s = math.cos(2 * math.pi * turn), math.sin(2 * math.pi * turn)
    if im is None:
        return (None, None) if re is None else (re * c, re * s)
    if re is None:
        return im * -s, im * c
    if eighth is not None:
        if eighth == 1:
            return (re - im) * c, (re + im) * c
        if eighth == 3:
            return (re + im) * c, (im - re) * -c
        if eighth == 5:
            return (re - im) * c, (re + im) * c
        return (re + im) * c, (im - re) * c
    return re * c - im * s, re * s + im * c


def real_dft(xs):
    n = len(xs)
    if n == 1:
        return [(xs[0], None)]
    even, odd = real_dft(xs[::2]), real_dft(xs[1::2])
    out = [None] * (n // 2 + 1)
    for k in range(n // 4 + 1):
        er, ei = even[k]
        rr, ri = rotate(odd[k], -k / n)
        out[k] = (add(er, rr), add(ei, ri))
        if n // 2 - k != k:
            dr, di = sub(er, rr), sub(ei, ri)
            out[n // 2 - k] = (dr, None if di is None else -di)
    return out


def real_inverse(hs):
    n = 2 * (len(hs) - 1)
    if n == 2:
        return [add(hs[0][0], hs[1][0])]
    even, odd = [], []
    for k in range(n // 4 + 1):
        ar, ai = hs[k]
        br, bi = hs[n // 2 - k]
        if k == n // 4:
            even.append((ar + ar, None))
            odd.append((-(ai + ai), None))
            continue
        even.append((add(ar, br), sub(ai, bi)))
        odd.append(rotate((sub(ar, br), add(ai, bi)), k / n))
    out = [None] * (n // 2)
    out[::2] = real_inverse(even)
    out[1::2] = real_inverse(odd)
    return out


def split_store(hi_ref, lo_ref, index, value):
    hi = value.astype(jnp.bfloat16)
    hi_ref[index] = hi
    lo_ref[index] = (value - hi.astype(jnp.float32)).astype(jnp.bfloat16)


def split(value):
    hi = value.astype(jnp.bfloat16)
    return hi, (value - hi.astype(jnp.float32)).astype(jnp.bfloat16)


def dot3(mat_hi, mat_lo, hi, lo):
    dot = partial(jnp.dot, preferred_element_type=jnp.float32)
    return dot(mat_hi, hi) + dot(mat_hi, lo) + dot(mat_lo, hi)


def local_kernel(outer, inner, v_ref, g_ref, o_ref, f_ref, s_ref, fh, fl, ih, il,
                 mixed_ref, ggate_ref, gval_ref, gfil_ref, ahi, alo, back):
    half = outer // 2
    width = v_ref.shape[1]
    k = pl.program_id(0)

    def spread(strip, _):
        row = pl.multiple_of(strip * STRIP, STRIP)

        def take(ref, a):
            return ref[pl.ds(pl.multiple_of(a * inner + row, STRIP), STRIP), :].astype(jnp.float32)

        signals = (
            [take(v_ref, a) for a in range(half)],
            [take(g_ref, a) * take(o_ref, a) for a in range(half)],
            [take(f_ref, a) for a in range(half)],
        )
        for which, blocks in enumerate(signals):
            cols = pl.ds(which * width, width)
            for freq, (re, im) in enumerate(real_dft(blocks + [None] * half)):
                split_store(ahi, alo, (freq, pl.ds(row, STRIP), cols), re)
                im = jnp.zeros_like(re) if im is None else im
                split_store(ahi, alo, (freq, pl.ds(pl.multiple_of(inner + row, STRIP), STRIP), cols), im)
        return 0

    @pl.when(k == 0)
    def _():
        lax.fori_loop(0, inner // STRIP, spread, 0)

    spec = dot3(fh[0], fl[0], ahi[k], alo[k])
    vr, gr, fr = (spec[:inner, i * width:(i + 1) * width] for i in range(3))
    vi, gi, fi = (spec[inner:, i * width:(i + 1) * width] for i in range(3))
    for i, (re, im) in enumerate((
        (vr * fr - vi * fi, vr * fi + vi * fr),
        (gr * fr + gi * fi, gi * fr - gr * fi),
        (gr * vr + gi * vi, gi * vr - gr * vi),
    )):
        hi, lo = split(jnp.concatenate([re, im], 0))
        back[k, :, pl.ds(i * width, width)] = dot3(ih[0], il[0], hi, lo)

    skip = s_ref[...]

    def gather(strip, _):
        row = pl.multiple_of(strip * STRIP, STRIP)

        def blocks_of(which):
            cols = pl.ds(which * width, width)
            hs = []
            for freq in range(half + 1):
                re = back[freq, pl.ds(row, STRIP), cols]
                if freq in (0, half):
                    hs.append((re, None))
                else:
                    hs.append((re, back[freq, pl.ds(pl.multiple_of(inner + row, STRIP), STRIP), cols]))
            return real_inverse(hs)

        def rows(a):
            return pl.ds(pl.multiple_of(a * inner + row, STRIP), STRIP)

        for a, conv in enumerate(blocks_of(0)):
            gate = g_ref[rows(a), :].astype(jnp.float32)
            grad = o_ref[rows(a), :].astype(jnp.float32)
            mixer = conv + skip * v_ref[rows(a), :].astype(jnp.float32)
            mixed_ref[rows(a), :] = (gate * mixer).astype(jnp.bfloat16)
            ggate_ref[rows(a), :] = (grad * mixer).astype(jnp.bfloat16)
        for a, conv in enumerate(blocks_of(1)):
            gm = g_ref[rows(a), :].astype(jnp.float32) * o_ref[rows(a), :].astype(jnp.float32)
            gval_ref[rows(a), :] = (conv + skip * gm).astype(jnp.bfloat16)
        for a, conv in enumerate(blocks_of(2)):
            gfil_ref[rows(a), :] = conv
        return 0

    @pl.when(k == half)
    def _():
        lax.fori_loop(0, inner // STRIP, gather, 0)


def local_mix(values, gates, grads, filters, skips):
    length, width = values.shape
    outer, inner = plan(length)
    pad = -width % LANES
    if pad:
        values, gates, grads, filters, skips = (
            jnp.pad(x, ((0, 0), (0, pad))) for x in (values, gates, grads, filters, skips)
        )
    full = width + pad
    half = outer // 2
    shape = (length, full)
    vmem = pl.BlockSpec(memory_space=pltpu.VMEM)
    table = pl.BlockSpec((1, 2 * inner, 2 * inner), lambda k: (k, 0, 0))
    outs = pl.pallas_call(
        partial(local_kernel, outer, inner),
        out_shape=[jax.ShapeDtypeStruct(shape, t) for t in (jnp.bfloat16,) * 3 + (jnp.float32,)],
        grid=(half + 1,),
        in_specs=[vmem] * 5 + [table] * 4,
        out_specs=[vmem] * 4,
        scratch_shapes=[
            pltpu.VMEM((half + 1, 2 * inner, 3 * full), jnp.bfloat16),
            pltpu.VMEM((half + 1, 2 * inner, 3 * full), jnp.bfloat16),
            pltpu.VMEM((half + 1, 2 * inner, 3 * full), jnp.float32),
        ],
        compiler_params=pltpu.CompilerParams(vmem_limit_bytes=(58 if pad else 40) * 2**20),
    )(values, gates, grads, filters, skips, *(jnp.asarray(t) for t in tables(length)))
    return [x[:, :width] for x in outs] if pad else outs


def on_device(values, gates, filters, skips, grad_out):
    rows, columns = values.shape
    group = lax.axis_size("context")
    width = columns // group
    to_channels = partial(lax.all_to_all, axis_name="context", split_axis=1, concat_axis=0, tiled=True)
    to_rows = partial(lax.all_to_all, axis_name="context", split_axis=0, concat_axis=1, tiled=True)
    mine = lax.dynamic_slice_in_dim(skips, lax.axis_index("context") * width, width, 0)
    mixed, ggate, gval, gfil = local_mix(
        to_channels(values), to_channels(gates), to_channels(grad_out), to_channels(filters), mine[None, :]
    )
    return to_rows(mixed), to_rows(ggate), to_rows(gval), to_rows(lax.psum(gfil, "dp"))


def solution(mesh):
    placed = (P("context", "dp"), P("context", "dp"), P("context", None), P("dp"), P("context", "dp"))
    return jax.shard_map(
        on_device,
        mesh=mesh,
        in_specs=placed,
        out_specs=(P("context", "dp"), P("context", "dp"), P("context", "dp"), P("context", None)),
        check_vma=False,
    )
```

profile of v0, /device:TPU:0, one launch (start us, length us, event | category | flops | bytes accessed | tf_op | source)
XLA Modules:
  0.0 172.8 jit_solution(12785316649131293744)
XLA Ops:
  7.2 0.0 copy-start
  7.2 0.0 copy-start.13
  7.2 0.0 copy-start.14
  7.2 1.8 %copy_bitcast_fusion.7 = bf16[256,4,128]{2,0,1:T(8,128)(2,1)} fusion(bf16[256,512]{1,0:T(8,128)(2,1)} %param.9), kind=kLoop, calls=%fused_computation.7 | loop fusion | bytes 524288 | tf_op jit(solution)/shard_map/all_to_all | solution.py:251
  9.0 4.2 %all-to-all-start = ((bf16[256,4,128]{2,0,1:T(8,128)(2,1)}), bf16[256,4,128]{2,0,1:T(8,128)(2,1)S(1)}, u32[]{:S(2)}, u32[]{:S(2)}) async-start(bf16[256,4,128]{2,0,1:T(8,128)(2,1)} %copy_bitcast_fusion.7), calls=%async_computation | async-start | bytes 524288 | tf_op jit(solution)/shard_map/all_to_all | solution.py:251
  13.2 0.0 copy-done.13
  13.2 0.7 copy_bitcast_fusion.6
  14.0 5.3 %all-to-all-done = bf16[256,4,128]{2,0,1:T(8,128)(2,1)S(1)} async-done(((bf16[256,4,128]{2,0,1:T(8,128)(2,1)}), bf16[256,4,128]{2,0,1:T(8,128)(2,1)S(1)}, u32[]{:S(2)}, u32[]{:S(2)}) %all-to-all-start) | async-done | bytes 262176 | tf_op jit(solution)/shard_map/all_to_all | solution.py:251
  19.3 0.0 copy-start.5
  19.3 3.4 %all-to-all-start.1 = ((bf16[256,4,128]{2,0,1:T(8,128)(2,1)}), bf16[256,4,128]{2,0,1:T(8,128)(2,1)S(1)}, u32[]{:S(2)}, u32[]{:S(2)}) async-start(bf16[256,4,128]{2,0,1:T(8,128)(2,1)} %copy_bitcast_fusion.6), calls=%async_computation.1 | async-start | bytes 524288 | tf_op jit(solution)/shard_map/all_to_all | solution.py:251
  22.7 0.0 copy-done.14
  22.7 0.7 copy_bitcast_fusion.5
  23.4 5.2 %all-to-all-done.1 = bf16[256,4,128]{2,0,1:T(8,128)(2,1)S(1)} async-done(((bf16[256,4,128]{2,0,1:T(8,128)(2,1)}), bf16[256,4,128]{2,0,1:T(8,128)(2,1)S(1)}, u32[]{:S(2)}, u32[]{:S(2)}) %all-to-all-start.1) | async-done | bytes 262176 | tf_op jit(solution)/shard_map/all_to_all | solution.py:251
  28.7 0.0 copy-start.7
  28.7 0.0 copy-start.2
  28.7 4.2 %all-to-all-start.2 = ((bf16[256,4,128]{2,0,1:T(8,128)(2,1)}), bf16[256,4,128]{2,0,1:T(8,128)(2,1)}, u32[]{:S(2)}, u32[]{:S(2)}) async-start(bf16[256,4,128]{2,0,1:T(8,128)(2,1)} %copy_bitcast_fusion.5), calls=%async_computation.2 | async-start | bytes 524288 | tf_op jit(solution)/shard_map/all_to_all | solution.py:251
  32.9 0.0 copy-done
  32.9 0.0 copy-start.1
  32.9 0.8 copy_bitcast_fusion.1
  33.7 0.0 copy-done.5
  33.7 5.2 %all-to-all-done.2 = bf16[256,4,128]{2,0,1:T(8,128)(2,1)} async-done(((bf16[256,4,128]{2,0,1:T(8,128)(2,1)}), bf16[256,4,128]{2,0,1:T(8,128)(2,1)}, u32[]{:S(2)}, u32[]{:S(2)}) %all-to-all-start.2) | async-done | bytes 262176 | tf_op jit(solution)/shard_map/all_to_all | solution.py:251
  39.0 0.0 copy-done.7
  39.0 3.5 %all-to-all-start.3 = ((f32[256,4,128]{2,0,1:T(8,128)}), f32[256,4,128]{2,0,1:T(8,128)S(1)}, u32[]{:S(2)}, u32[]{:S(2)}) async-start(f32[256,4,128]{2,0,1:T(8,128)} %copy_bitcast_fusion.1), calls=%async_computation.3 | async-start | bytes 1048576 | tf_op jit(solution)/shard_map/all_to_all | solution.py:251
  42.5 0.8 dynamic-slice_bitcast_fusion.s_ref
  43.2 8.0 %all-to-all-done.3 = f32[256,4,128]{2,0,1:T(8,128)S(1)} async-done(((f32[256,4,128]{2,0,1:T(8,128)}), f32[256,4,128]{2,0,1:T(8,128)S(1)}, u32[]{:S(2)}, u32[]{:S(2)}) %all-to-all-start.3) | async-done | bytes 524320 | tf_op jit(solution)/shard_map/all_to_all | solution.py:251
  51.3 0.0 copy-done.2
  51.3 0.0 copy-done.1
  51.3 0.0 copy-start.3
  51.3 1.3 copy-done.3
  52.5 0.0 copy-start.4
  52.5 1.3 copy-done.4
  53.8 0.0 copy-start.6
  53.8 0.9 copy-done.6
  54.8 0.0 copy-start.8
  54.8 0.9 copy-done.8
  55.7 11.9 %shard_map.120 = (bf16[1024,128]{1,0:T(8,128)(2,1)S(1)}, bf16[1024,128]{1,0:T(8,128)(2,1)S(1)}, bf16[1024,128]{1,0:T(8,128)(2,1)}, f32[1024,128]{1,0:T(8,128)S(1)}) custom-call(bf16[1024,128]{1,0:T(8,128)(2,1)S(1)} %bitcast.63, bf16[1024,128]{1,0:T(8,128)(2,1)S(1)} %bitcast.64, bf16[1024,128]{1,0:T(8,128)(2,1)} %bitcast.5.o_ref, f32[1024,128]{1,0:T(8,128)S(1)} %bitcast.62, ...), custom_call_target="tpu_custom_call" | custom-call | tf_op jit(solution)/shard_map/pallas_call | solution.py:227
  67.6 0.0 copy-start.9
  67.6 0.8 copy-done.9
  68.4 0.0 copy-start.10
  68.4 0.7 copy-done.10
  69.1 0.0 copy-start.12
  69.1 0.7 copy-done.12
  69.8 0.0 copy-start.11
  69.8 3.5 %all-to-all-start.5 = ((bf16[4,256,128]{2,1,0:T(8,128)(2,1)}), bf16[4,256,128]{2,1,0:T(8,128)(2,1)S(1)}, u32[]{:S(2)}, u32[]{:S(2)}) async-start(bf16[4,256,128]{2,1,0:T(8,128)(2,1)} %bitcast.67), calls=%async_computation.5 | async-start | bytes 524288 | tf_op jit(solution)/shard_map/all_to_all | solution.py:253
  73.3 0.0 all-reduce.2.cloned.1.call-start
  73.4 0.7 all-reduce.2.cloned.1.call-update
  74.1 5.3 %all-to-all-done.5 = bf16[4,256,128]{2,1,0:T(8,128)(2,1)S(1)} async-done(((bf16[4,256,128]{2,1,0:T(8,128)(2,1)}), bf16[4,256,128]{2,1,0:T(8,128)(2,1)S(1)}, u32[]{:S(2)}, u32[]{:S(2)}) %all-to-all-start.5) | async-done | bytes 262176 | tf_op jit(solution)/shard_map/all_to_all | solution.py:253
  79.3 0.0 copy-done.11
  79.3 8.4 %all_to_all.152 = bf16[4,256,128]{2,1,0:T(8,128)(2,1)S(1)} all-to-all(bf16[4,256,128]{2,1,0:T(8,128)(2,1)S(1)} %bitcast.66), channel_id=1, replica_groups=mesh['dp'=8,'context'=4] {'context'}, dimensions={0} | all-to-all | bytes 524288 | tf_op jit(solution)/shard_map/all_to_all | solution.py:253
  87.7 3.4 %all-to-all-start.6 = ((bf16[4,256,128]{2,1,0:T(8,128)(2,1)}), bf16[4,256,128]{2,1,0:T(8,128)(2,1)S(1)}, u32[]{:S(2)}, u32[]{:S(2)}) async-start(bf16[4,256,128]{2,1,0:T(8,128)(2,1)} %bitcast.13), calls=%async_computation.6 | async-start | bytes 524288 | tf_op jit(solution)/shard_map/all_to_all | solution.py:253
  91.2 0.7 copy_bitcast_fusion.3
  91.9 5.3 %all-to-all-done.6 = bf16[4,256,128]{2,1,0:T(8,128)(2,1)S(1)} async-done(((bf16[4,256,128]{2,1,0:T(8,128)(2,1)}), bf16[4,256,128]{2,1,0:T(8,128)(2,1)S(1)}, u32[]{:S(2)}, u32[]{:S(2)}) %all-to-all-start.6) | async-done | bytes 262176 | tf_op jit(solution)/shard_map/all_to_all | solution.py:253
  97.2 55.6 %all-reduce.2.cloned.1.call-done = f32[4,256,128]{2,1,0:T(8,128)} async-done(((f32[4,256,128]{2,1,0:T(8,128)}), f32[4,256,128]{2,1,0:T(8,128)}) %all-reduce.2.cloned.1.call-update) | async-done | bytes 524304 | tf_op jit(solution)/shard_map/psum | solution.py:253
  152.8 3.5 %all-to-all-start.7 = ((f32[4,256,128]{2,1,0:T(8,128)}), f32[4,256,128]{2,1,0:T(8,128)S(1)}, u32[]{:S(2)}, u32[]{:S(2)}) async-start(f32[4,256,128]{2,1,0:T(8,128)} %all-reduce.2.cloned.1.call-done), calls=%async_computation.7 | async-start | bytes 1048576 | tf_op jit(solution)/shard_map/all_to_all | solution.py:253
  156.3 0.7 copy_bitcast_fusion.4
  157.0 0.7 copy_bitcast_fusion.2
  157.7 7.3 %all-to-all-done.7 = f32[4,256,128]{2,1,0:T(8,128)S(1)} async-done(((f32[4,256,128]{2,1,0:T(8,128)}), f32[4,256,128]{2,1,0:T(8,128)S(1)}, u32[]{:S(2)}, u32[]{:S(2)}) %all-to-all-start.7) | async-done | bytes 524320 | tf_op jit(solution)/shard_map/all_to_all | solution.py:253
  165.1 0.9 copy_bitcast_fusion
Async XLA Ops:
  7.2 25.7 %copy-start = (f32[256,512]{1,0:T(8,128)S(1)}, f32[256,512]{1,0:T(8,128)}, u32[]{:S(2)}) copy-start(f32[256,512]{1,0:T(8,128)} %param.11) | copy-start | bytes 1572868
  7.2 6.0 %copy-start.13 = (bf16[256,512]{1,0:T(8,128)(2,1)S(1)}, bf16[256,512]{1,0:T(8,128)(2,1)}, u32[]{:S(2)}) copy-start(bf16[256,512]{1,0:T(8,128)(2,1)} %param.10) | copy-start | bytes 786436
  7.2 15.5 %copy-start.14 = (bf16[256,512]{1,0:T(8,128)(2,1)S(1)}, bf16[256,512]{1,0:T(8,128)(2,1)}, u32[]{:S(2)}) copy-start(bf16[256,512]{1,0:T(8,128)(2,1)} %param.13) | copy-start | bytes 786436
  9.0 10.3 %all-to-all-start = ((bf16[256,4,128]{2,0,1:T(8,128)(2,1)}), bf16[256,4,128]{2,0,1:T(8,128)(2,1)S(1)}, u32[]{:S(2)}, u32[]{:S(2)}) async-start(bf16[256,4,128]{2,0,1:T(8,128)(2,1)} %copy_bitcast_fusion.7), calls=%async_computation | async-start | bytes 524288 | tf_op jit(solution)/shard_map/all_to_all | solution.py:251
  19.3 14.5 %copy-start.5 = (bf16[256,4,128]{2,0,1:T(8,128)(2,1)}, bf16[256,4,128]{2,0,1:T(8,128)(2,1)S(1)}, u32[]{:S(2)}) copy-start(bf16[256,4,128]{2,0,1:T(8,128)(2,1)S(1)} %all-to-all-done) | copy-start | bytes 786436
  19.3 9.4 %all-to-all-start.1 = ((bf16[256,4,128]{2,0,1:T(8,128)(2,1)}), bf16[256,4,128]{2,0,1:T(8,128)(2,1)S(1)}, u32[]{:S(2)}, u32[]{:S(2)}) async-start(bf16[256,4,128]{2,0,1:T(8,128)(2,1)} %copy_bitcast_fusion.6), calls=%async_computation.1 | async-start | bytes 524288 | tf_op jit(solution)/shard_map/all_to_all | solution.py:251
  28.7 10.3 %copy-start.7 = (bf16[256,4,128]{2,0,1:T(8,128)(2,1)}, bf16[256,4,128]{2,0,1:T(8,128)(2,1)S(1)}, u32[]{:S(2)}) copy-start(bf16[256,4,128]{2,0,1:T(8,128)(2,1)S(1)} %all-to-all-done.1) | copy-start | bytes 786436
  28.7 22.6 %copy-start.2 = (bf16[9,256,256]{2,1,0:T(8,128)(2,1)S(1)}, bf16[9,256,256]{2,1,0:T(8,128)(2,1)}, u32[]{:S(2)}) copy-start(bf16[9,256,256]{2,1,0:T(8,128)(2,1)} %constant.20.clone.ih) | copy-start | bytes 3538948
  28.7 10.3 %all-to-all-start.2 = ((bf16[256,4,128]{2,0,1:T(8,128)(2,1)}), bf16[256,4,128]{2,0,1:T(8,128)(2,1)}, u32[]{:S(2)}, u32[]{:S(2)}) async-start(bf16[256,4,128]{2,0,1:T(8,128)(2,1)} %copy_bitcast_fusion.5), calls=%async_computation.2 | async-start | bytes 524288 | tf_op jit(solution)/shard_map/all_to_all | solution.py:251
  32.9 18.4 %copy-start.1 = (bf16[9,256,256]{2,1,0:T(8,128)(2,1)S(1)}, bf16[9,256,256]{2,1,0:T(8,128)(2,1)}, u32[]{:S(2)}) copy-start(bf16[9,256,256]{2,1,0:T(8,128)(2,1)} %constant.21.clone.il) | copy-start | bytes 3538948
  39.0 12.3 %all-to-all-start.3 = ((f32[256,4,128]{2,0,1:T(8,128)}), f32[256,4,128]{2,0,1:T(8,128)S(1)}, u32[]{:S(2)}, u32[]{:S(2)}) async-start(f32[256,4,128]{2,0,1:T(8,128)} %copy_bitcast_fusion.1), calls=%async_computation.3 | async-start | bytes 1048576 | tf_op jit(solution)/shard_map/all_to_all | solution.py:251
  51.3 1.3 copy-start.3
  52.5 1.3 copy-start.4
  53.8 0.9 copy-start.6
  54.8 0.9 copy-start.8
  67.6 0.8 copy-start.9
  68.4 0.7 copy-start.10
  69.1 0.7 copy-start.12
  69.8 9.6 %copy-start.11 = (bf16[1024,128]{1,0:T(8,128)(2,1)S(1)}, bf16[1024,128]{1,0:T(8,128)(2,1)}, u32[]{:S(2)}) copy-start(bf16[1024,128]{1,0:T(8,128)(2,1)} %copy-done.10) | copy-start | bytes 786436
  69.8 9.5 %all-to-all-start.5 = ((bf16[4,256,128]{2,1,0:T(8,128)(2,1)}), bf16[4,256,128]{2,1,0:T(8,128)(2,1)S(1)}, u32[]{:S(2)}, u32[]{:S(2)}) async-start(bf16[4,256,128]{2,1,0:T(8,128)(2,1)} %bitcast.67), calls=%async_computation.5 | async-start | bytes 524288 | tf_op jit(solution)/shard_map/all_to_all | solution.py:253
  73.3 79.5 %all-reduce.2.cloned.1.call-start = ((), (), s32[]{:S(2)}) async-start(), calls=%async_computation.8 | async-start | bytes 1048576 | tf_op jit(solution)/shard_map/psum | solution.py:253
  87.7 9.4 %all-to-all-start.6 = ((bf16[4,256,128]{2,1,0:T(8,128)(2,1)}), bf16[4,256,128]{2,1,0:T(8,128)(2,1)S(1)}, u32[]{:S(2)}, u32[]{:S(2)}) async-start(bf16[4,256,128]{2,1,0:T(8,128)(2,1)} %bitcast.13), calls=%async_computation.6 | async-start | bytes 524288 | tf_op jit(solution)/shard_map/all_to_all | solution.py:253
  152.8 12.3 %all-to-all-start.7 = ((f32[4,256,128]{2,1,0:T(8,128)}), f32[4,256,128]{2,1,0:T(8,128)S(1)}, u32[]{:S(2)}, u32[]{:S(2)}) async-start(f32[4,256,128]{2,1,0:T(8,128)} %all-reduce.2.cloned.1.call-done), calls=%async_computation.7 | async-start | bytes 1048576 | tf_op jit(solution)/shard_map/all_to_all | solution.py:253
Sparse Core Ops, SparseCore 0:
  78.1 74.5 all-reduce.1
where the time goes:
time: 174 us; the launch traced here: 173 us
  waiting for transfers between devices  98 us (56%)
  starting transfers between devices  25.7 us (15%)
  local copies, waits for them, and re-layouts  14.6 us (8%)
  between operations  14.1 us (8%)
  Pallas kernels  11.9 us (7%)
  blocking collectives  8.41 us (5%)
    psum x1, waiting for transfers between devices, on_device(): lax.psum(gfil, 'dp')  55.6 us
    pallas_call x1, Pallas kernels, local_mix(): pl.pallas_call(partial(local_kernel, outer, inner), out_shape=[jax.ShapeD...  11.9 us
    all_to_all x1, blocking collectives, on_device(): to_rows(mixed)  8.41 us
    all_to_all x1, waiting for transfers between devices, on_device(): to_channels(filters)  8.05 us
    all_to_all x1, waiting for transfers between devices, on_device(): to_rows(lax.psum(gfil, 'dp'))  7.35 us
    unnamed x30, local copies, waits for them, and re-layouts  6.68 us
    all_to_all x1, waiting for transfers between devices, on_device(): to_channels(values)  5.29 us
    all_to_all x1, waiting for transfers between devices, on_device(): to_rows(gval)  5.27 us
  transfers between devices with their start and end apart: 8, of which 8 were waited for; matrix products, arithmetic and copies ran while one was open for 3% of the time, Pallas kernels for 0%

commit v1 on v0

--- a/solution.py
+++ b/solution.py
@@ -11,6 +11,7 @@
 
 LANES = 128
 STRIP = 16
+MESH = pl.DeviceIdType.MESH
 
 
 def plan(length):
@@ -240,6 +241,329 @@
     return [x[:, :width] for x in outs] if pad else outs
 
 
+def fused_kernel(outer, inner, n_dp, n_ctx, v_in, g_in, o_in, f_in, s_ref, fh_in, fl_in, ih_in, il_in,
+                 mixed_out, ggate_out, gval_out, gfil_out,
+                 v_ref, g_ref, o_ref, f_ref, fh, fl, ih, il, ahi, alo, spec, back,
+                 mixed_ref, ggate_ref, gval_ref, gfil_ref, rs_buf, piece,
+                 tab_sem, own_sem, in_send, in_recv, out_send, out_recv,
+                 rs_send, rs_recv, pc_send, pc_recv, bc_send, bc_recv):
+    half = outer // 2
+    length, width = v_ref.shape
+    rows_here = length // n_ctx
+    rows_piece = length // n_dp
+    dp, ctx = lax.axis_index("dp"), lax.axis_index("context")
+    f32 = jnp.float32
+    dot = partial(jnp.dot, preferred_element_type=f32)
+
+    def ctx_at(step):
+        return lax.rem(ctx + step + n_ctx, n_ctx)
+
+    def dp_at(step):
+        return lax.rem(dp + step + n_dp, n_dp)
+
+    def block_rows(p):
+        return pl.ds(pl.multiple_of(p * rows_here, 16), rows_here)
+
+    def block_cols(p):
+        return pl.ds(pl.multiple_of(p * width, LANES), width)
+
+    loads = [
+        pltpu.make_async_copy(src, dst, tab_sem.at[i])
+        for i, (src, dst) in enumerate(((fh_in, fh), (fl_in, fl), (ih_in, ih), (il_in, il)))
+    ]
+    arrays = ((v_in, v_ref), (g_in, g_ref), (o_in, o_ref), (f_in, f_ref))
+    own = [
+        pltpu.make_async_copy(src.at[:, block_cols(ctx)], dst.at[block_rows(ctx), :], own_sem.at[i])
+        for i, (src, dst) in enumerate(arrays)
+    ]
+    for copy in own + loads:
+        copy.start()
+
+    barrier = pltpu.get_barrier_semaphore()
+    for step in range(1, n_ctx):
+        pl.semaphore_signal(barrier, inc=1, device_id={"context": ctx_at(step)}, device_id_type=MESH)
+    for step in range(1, n_dp):
+        pl.semaphore_signal(barrier, inc=1, device_id={"dp": dp_at(step)}, device_id_type=MESH)
+    pl.semaphore_wait(barrier, n_ctx - 1 + n_dp - 1)
+
+    def inbound(i, step):
+        src, dst = arrays[i]
+        return pltpu.make_async_remote_copy(
+            src_ref=src.at[:, block_cols(ctx_at(step))],
+            dst_ref=dst.at[block_rows(ctx_at(-step)), :],
+            send_sem=in_send.at[i, step],
+            recv_sem=in_recv.at[i, step],
+            device_id={"context": ctx_at(step)},
+            device_id_type=MESH,
+        )
+
+    def outbound_in(i, step):
+        src, dst = arrays[i]
+        return pltpu.make_async_remote_copy(
+            src_ref=src.at[:, block_cols(ctx_at(step))],
+            dst_ref=dst.at[block_rows(ctx), :],
+            send_sem=in_send.at[i, step],
+            recv_sem=in_recv.at[i, step],
+            device_id={"context": ctx_at(step)},
+            device_id_type=MESH,
+        )
+
+    for i in range(4):
+        for step in range(1, n_ctx):
+            outbound_in(i, step).start()
+
+    def arrived(i):
+        own[i].wait()
+        for step in range(1, n_ctx):
+            inbound(i, step).wait_recv()
+
+    def take(ref, a, row):
+        return ref[pl.ds(pl.multiple_of(a * inner + row, STRIP), STRIP), :].astype(f32)
+
+    def spread(which, blocks, row):
+        cols = pl.ds(which * width, width)
+        for freq, (re, im) in enumerate(real_dft(blocks + [None] * half)):
+            split_store(ahi, alo, (freq, pl.ds(row, STRIP), cols), re)
+            im = jnp.zeros_like(re) if im is None else im
+            split_store(ahi, alo, (freq, pl.ds(pl.multiple_of(inner + row, STRIP), STRIP), cols), im)
+
+    def gather(which, row):
+        cols = pl.ds(which * width, width)
+        hs = []
+        for freq in range(half + 1):
+            re = back[freq, pl.ds(row, STRIP), cols]
+            if freq in (0, half):
+                hs.append((re, None))
+            else:
+                hs.append((re, back[freq, pl.ds(pl.multiple_of(inner + row, STRIP), STRIP), cols]))
+        return real_inverse(hs)
+
+    def strips(body):
+        def run(strip, carry):
+            body(pl.multiple_of(strip * STRIP, STRIP))
+            return carry
+
+        lax.fori_loop(0, inner // STRIP, run, 0)
+
+    def invert(k, which, re, im):
+        hi, lo = split(jnp.concatenate([re, im], 0))
+        back[k, :, pl.ds(which * width, width)] = dot3(ih[k], il[k], hi, lo)
+
+    arrived(0)
+
+    def spread_values(row):
+        spread(0, [take(v_ref, a, row) for a in range(half)], row)
+
+    strips(spread_values)
+    arrived(1)
+    arrived(2)
+
+    def spread_grads(row):
+        spread(1, [take(g_ref, a, row) * take(o_ref, a, row) for a in range(half)], row)
+
+    strips(spread_grads)
+    for copy in loads:
+        copy.wait()
+
+    def first(k, carry):
+        both = dot3(fh[k], fl[k], ahi[k, :, : 2 * width], alo[k, :, : 2 * width])
+        spec[k] = both
+        vr, gr = both[:inner, :width], both[:inner, width:]
+        vi, gi = both[inner:, :width], both[inner:, width:]
+        invert(k, 2, gr * vr + gi * vi, gi * vr - gr * vi)
+        return carry
+
+    lax.fori_loop(0, half + 1, first, 0)
+
+    def gather_filters(row):
+        for a, conv in enumerate(gather(2, row)):
+            gfil_ref[pl.ds(pl.multiple_of(a * inner + row, STRIP), STRIP), :] = conv
+
+    strips(gather_filters)
+
+    def piece_rows(d):
+        place = lax.rem(d, n_ctx) * (n_dp // n_ctx) + d // n_ctx
+        return pl.ds(pl.multiple_of(place * rows_piece, 8), rows_piece)
+
+    scatter = [
+        pltpu.make_async_remote_copy(
+            src_ref=gfil_ref.at[piece_rows(dp_at(step)), :],
+            dst_ref=rs_buf.at[step],
+            send_sem=rs_send.at[step],
+            recv_sem=rs_recv.at[step],
+            device_id={"dp": dp_at(step)},
+            device_id_type=MESH,
+        )
+        for step in range(1, n_dp)
+    ]
+    for copy in scatter:
+        copy.start()
+
+    arrived(3)
+
+    def spread_filters(row):
+        spread(2, [take(f_ref, a, row) for a in range(half)], row)
+
+    strips(spread_filters)
+
+    def second(k, carry):
+        filt = dot3(fh[k], fl[k], ahi[k, :, 2 * width:], alo[k, :, 2 * width:])
+        fr, fi = filt[:inner], filt[inner:]
+        both = spec[k]
+        vr, gr = both[:inner, :width], both[:inner, width:]
+        vi, gi = both[inner:, :width], both[inner:, width:]
+        invert(k, 0, vr * fr - vi * fi, vr * fi + vi * fr)
+        invert(k, 1, gr * fr + gi * fi, gi * fr - gr * fi)
+        return carry
+
+    lax.fori_loop(0, half + 1, second, 0)
+    skip = s_ref[...]
+
+    def finish(row):
+        def rows(a):
+            return pl.ds(pl.multiple_of(a * inner + row, STRIP), STRIP)
+
+        for a, conv in enumerate(gather(0, row)):
+            gate, grad = take(g_ref, a, row), take(o_ref, a, row)
+            mixer = conv + skip * take(v_ref, a, row)
+            mixed_ref[rows(a), :] = (gate * mixer).astype(jnp.bfloat16)
+            ggate_ref[rows(a), :] = (grad * mixer).astype(jnp.bfloat16)
+        for a, conv in enumerate(gather(1, row)):
+            gm = take(g_ref, a, row) * take(o_ref, a, row)
+            gval_ref[rows(a), :] = (conv + skip * gm).astype(jnp.bfloat16)
+
+    strips(finish)
+
+    results = ((mixed_ref, mixed_out), (ggate_ref, ggate_out), (gval_ref, gval_out))
+
+    def returned(i, step, landing):
+        src, dst = results[i]
+        return pltpu.make_async_remote_copy(
+            src_ref=src.at[block_rows(ctx_at(step)), :],
+            dst_ref=dst.at[:, block_cols(landing)],
+            send_sem=out_send.at[i, step],
+            recv_sem=out_recv.at[i, step],
+            device_id={"context": ctx_at(step)},
+            device_id_type=MESH,
+        )
+
+    for i in range(3):
+        for step in range(1, n_ctx):
+            returned(i, step, ctx).start()
+    kept = [
+        pltpu.make_async_copy(src.at[block_rows(ctx), :], dst.at[:, block_cols(ctx)], own_sem.at[i])
+        for i, (src, dst) in enumerate(results)
+    ]
+    for copy in kept:
+        copy.start()
+
+    total = gfil_ref[piece_rows(dp), :]
+    for step, copy in zip(range(1, n_dp), scatter):
+        copy.wait_recv()
+        total = total + rs_buf[step]
+    piece[:, block_cols(ctx)] = total
+
+    holder = lax.rem(dp, n_ctx)
+    part = dp // n_ctx
+    gap = lax.rem(ctx - holder + n_ctx, n_ctx)
+
+    def part_rows(j):
+        return pl.ds(pl.multiple_of(j * rows_piece, 8), rows_piece)
+
+    def collect(which, c):
+        return pltpu.make_async_remote_copy(
+            src_ref=piece.at[:, block_cols(c)],
+            dst_ref=piece.at[:, block_cols(c)],
+            send_sem=pc_send.at[which],
+            recv_sem=pc_recv.at[which],
+            device_id={"context": holder},
+            device_id_type=MESH,
+        )
+
+    def cast(step, j):
+        return pltpu.make_async_remote_copy(
+            src_ref=piece,
+            dst_ref=gfil_out.at[part_rows(j), :],
+            send_sem=bc_send.at[step],
+            recv_sem=bc_recv.at[j],
+            device_id={"dp": dp_at(step)},
+            device_id_type=MESH,
+        )
+
+    @pl.when(ctx != holder)
+    def _():
+        copy = collect(gap, ctx)
+        copy.start()
+        copy.wait_send()
+
+    @pl.when(ctx == holder)
+    def _():
+        for step in range(1, n_ctx):
+            collect(step, ctx_at(step)).wait_recv()
+        for step in range(1, n_dp):
+            cast(step, part).start()
+        mine = pltpu.make_async_copy(piece, gfil_out.at[part_rows(part), :], own_sem.at[3])
+        mine.start()
+        mine.wait()
+        for step in range(1, n_dp):
+            cast(step, part).wait_send()
+
+    for j in range(n_dp // n_ctx):
+        @pl.when(dp != ctx + j * n_ctx)
+        def _():
+            cast(1, j).wait_recv()
+
+    for copy in kept:
+        copy.wait()
+    for i in range(3):
+        for step in range(1, n_ctx):
+            returned(i, step, ctx_at(-step)).wait_recv()
+            returned(i, step, ctx).wait_send()
+    for i in range(4):
+        for step in range(1, n_ctx):
+            outbound_in(i, step).wait_send()
+    for copy in scatter:
+        copy.wait_send()
+
+
+def fused(values, gates, grads, filters, skips, n_dp, n_ctx):
+    rows, columns = values.shape
+    length, width = rows * n_ctx, columns // n_ctx
+    outer, inner = plan(length)
+    half = outer // 2
+    vmem = pl.BlockSpec(memory_space=pltpu.VMEM)
+    anywhere = pl.BlockSpec(memory_space=pl.ANY)
+    bf16, f32 = jnp.bfloat16, jnp.float32
+    full = (length, width)
+    mats = (half + 1, 2 * inner, 2 * inner)
+    rows_piece = length // n_dp
+    dma = pltpu.SemaphoreType.DMA
+    return pl.pallas_call(
+        partial(fused_kernel, outer, inner, n_dp, n_ctx),
+        out_shape=[jax.ShapeDtypeStruct((rows, columns), t) for t in (bf16, bf16, bf16, f32)],
+        in_specs=[anywhere] * 4 + [vmem] + [anywhere] * 4,
+        out_specs=[anywhere] * 4,
+        scratch_shapes=[pltpu.VMEM(full, t) for t in (bf16, bf16, bf16, f32)]
+        + [pltpu.VMEM(mats, bf16)] * 4
+        + [
+            pltpu.VMEM((half + 1, 2 * inner, 3 * width), bf16),
+            pltpu.VMEM((half + 1, 2 * inner, 3 * width), bf16),
+            pltpu.VMEM((half + 1, 2 * inner, 2 * width), f32),
+            pltpu.VMEM((half + 1, 2 * inner, 3 * width), f32),
+        ]
+        + [pltpu.VMEM(full, t) for t in (bf16, bf16, bf16, f32)]
+        + [
+            pltpu.VMEM((n_dp, rows_piece, width), f32),
+            pltpu.VMEM((rows_piece, columns), f32),
+            dma((4,)), dma((4,)), dma((4, n_ctx)), dma((4, n_ctx)), dma((3, n_ctx)), dma((3, n_ctx)),
+            dma((n_dp,)), dma((n_dp,)), dma((n_ctx,)), dma((n_ctx,)), dma((n_dp,)), dma((n_dp // n_ctx,)),
+        ],
+        compiler_params=pltpu.CompilerParams(
+            collective_id=0, has_side_effects=True, vmem_limit_bytes=48 * 2**20
+        ),
+    )(values, gates, grads, filters, skips, *(jnp.asarray(t) for t in tables(length)))
+
+
 def on_device(values, gates, filters, skips, grad_out):
     rows, columns = values.shape
     group = lax.axis_size("context")
@@ -247,6 +571,9 @@
     to_channels = partial(lax.all_to_all, axis_name="context", split_axis=1, concat_axis=0, tiled=True)
     to_rows = partial(lax.all_to_all, axis_name="context", split_axis=0, concat_axis=1, tiled=True)
     mine = lax.dynamic_slice_in_dim(skips, lax.axis_index("context") * width, width, 0)
+    n_dp = lax.axis_size("dp")
+    if width % LANES == 0 and n_dp % group == 0:
+        return tuple(fused(values, gates, grad_out, filters, mine[None, :], n_dp, group))
     mixed, ggate, gval, gfil = local_mix(
         to_channels(values), to_channels(gates), to_channels(grad_out), to_channels(filters), mine[None, :]
     )

time: 174 us -> 73.3 us (0.42)
  the two profiles are of different devices: /device:TPU:0 before, /device:TPU:26 now
where the time goes in v1:
time: 73.3 us; the launch traced here: 72.1 us
  Pallas kernels  60.1 us (82%)
  local copies, waits for them, and re-layouts  11.4 us (16%)
    pallas_call x1, Pallas kernels, fused(): pl.pallas_call(partial(fused_kernel, outer, inner, n_dp, n_ctx), out_shap...  60.1 us
    unnamed x20, local copies, waits for them, and re-layouts  11.3 us

profile of v1, /device:TPU:26, one launch (start us, length us, event | category | flops | bytes accessed | tf_op | source)
XLA Modules:
  0.0 72.1 jit_solution(4588950668786597529)
XLA Ops:
  0.6 0.0 copy-start
  0.6 0.7 copy-done
  1.3 0.1 dynamic-slice_bitcast_fusion.s_ref
  1.4 0.0 copy-start.1
  1.4 1.3 %copy-done.1 = bf16[9,256,256]{2,1,0:T(8,128)(2,1)S(1)} copy-done((bf16[9,256,256]{2,1,0:T(8,128)(2,1)S(1)}, bf16[9,256,256]{2,1,0:T(8,128)(2,1)}, u32[]{:S(2)}) %copy-start.1) | copy-done | bytes 1179672
  2.7 0.0 copy-start.2
  2.7 1.3 %copy-done.2 = bf16[9,256,256]{2,1,0:T(8,128)(2,1)S(1)} copy-done((bf16[9,256,256]{2,1,0:T(8,128)(2,1)S(1)}, bf16[9,256,256]{2,1,0:T(8,128)(2,1)}, u32[]{:S(2)}) %copy-start.2) | copy-done | bytes 1179672
  3.9 0.0 copy-start.3
  3.9 1.3 %copy-done.3 = bf16[9,256,256]{2,1,0:T(8,128)(2,1)S(1)} copy-done((bf16[9,256,256]{2,1,0:T(8,128)(2,1)S(1)}, bf16[9,256,256]{2,1,0:T(8,128)(2,1)}, u32[]{:S(2)}) %copy-start.3) | copy-done | bytes 1179672
  5.2 0.0 copy-start.4
  5.2 1.0 %copy-done.4 = f32[256,512]{1,0:T(8,128)S(1)} copy-done((f32[256,512]{1,0:T(8,128)S(1)}, f32[256,512]{1,0:T(8,128)}, u32[]{:S(2)}) %copy-start.4) | copy-done | bytes 524312
  6.2 0.0 copy-start.5
  6.2 0.9 %copy-done.5 = bf16[256,512]{1,0:T(8,128)(2,1)S(1)} copy-done((bf16[256,512]{1,0:T(8,128)(2,1)S(1)}, bf16[256,512]{1,0:T(8,128)(2,1)}, u32[]{:S(2)}) %copy-start.5) | copy-done | bytes 262168
  7.2 0.0 copy-start.6
  7.2 0.9 %copy-done.6 = bf16[256,512]{1,0:T(8,128)(2,1)S(1)} copy-done((bf16[256,512]{1,0:T(8,128)(2,1)S(1)}, bf16[256,512]{1,0:T(8,128)(2,1)}, u32[]{:S(2)}) %copy-start.6) | copy-done | bytes 262168
  8.1 0.0 copy-start.7
  8.2 0.9 %copy-done.7 = bf16[256,512]{1,0:T(8,128)(2,1)S(1)} copy-done((bf16[256,512]{1,0:T(8,128)(2,1)S(1)}, bf16[256,512]{1,0:T(8,128)(2,1)}, u32[]{:S(2)}) %copy-start.7) | copy-done | bytes 262168
  9.1 60.1 %shard_map.120 = (bf16[256,512]{1,0:T(8,128)(2,1)S(1)}, bf16[256,512]{1,0:T(8,128)(2,1)S(1)}, bf16[256,512]{1,0:T(8,128)(2,1)S(1)}, f32[256,512]{1,0:T(8,128)S(1)}) custom-call(bf16[256,512]{1,0:T(8,128)(2,1)S(1)} %copy-done.5, bf16[256,512]{1,0:T(8,128)(2,1)S(1)} %copy-done.6, bf16[256,512]{1,0:T(8,128)(2,1)S(1)} %copy-done.7, f32[256,512]{1,0:T(8,128)S(1)} %copy-done.4, ...), custom_call_target="tpu_custom_call" | custom-call | tf_op jit(solution)/shard_map/pallas_call | solution.py:541
  69.2 0.7 copy.17
  70.0 0.7 copy.18
  70.7 0.7 copy.19
  71.4 0.8 %copy.20 = f32[256,512]{1,0:T(8,128)} copy(f32[256,512]{1,0:T(8,128)S(1)} %get-tuple-element.11) | data formatting | bytes 1048576
Async XLA Ops:
  0.6 0.7 copy-start
  1.4 1.3 %copy-start.1 = (bf16[9,256,256]{2,1,0:T(8,128)(2,1)S(1)}, bf16[9,256,256]{2,1,0:T(8,128)(2,1)}, u32[]{:S(2)}) copy-start(bf16[9,256,256]{2,1,0:T(8,128)(2,1)} %constant.20.clone.ih_in) | copy-start | bytes 3538948
  2.7 1.3 %copy-start.2 = (bf16[9,256,256]{2,1,0:T(8,128)(2,1)S(1)}, bf16[9,256,256]{2,1,0:T(8,128)(2,1)}, u32[]{:S(2)}) copy-start(bf16[9,256,256]{2,1,0:T(8,128)(2,1)} %constant.19.clone.fl_in) | copy-start | bytes 3538948
  3.9 1.3 %copy-start.3 = (bf16[9,256,256]{2,1,0:T(8,128)(2,1)S(1)}, bf16[9,256,256]{2,1,0:T(8,128)(2,1)}, u32[]{:S(2)}) copy-start(bf16[9,256,256]{2,1,0:T(8,128)(2,1)} %constant.18.clone.fh_in) | copy-start | bytes 3538948
  5.2 1.0 %copy-start.4 = (f32[256,512]{1,0:T(8,128)S(1)}, f32[256,512]{1,0:T(8,128)}, u32[]{:S(2)}) copy-start(f32[256,512]{1,0:T(8,128)} %f_in.1) | copy-start | bytes 1572868
  6.2 0.9 %copy-start.5 = (bf16[256,512]{1,0:T(8,128)(2,1)S(1)}, bf16[256,512]{1,0:T(8,128)(2,1)}, u32[]{:S(2)}) copy-start(bf16[256,512]{1,0:T(8,128)(2,1)} %v_in.1) | copy-start | bytes 786436
  7.2 0.9 %copy-start.6 = (bf16[256,512]{1,0:T(8,128)(2,1)S(1)}, bf16[256,512]{1,0:T(8,128)(2,1)}, u32[]{:S(2)}) copy-start(bf16[256,512]{1,0:T(8,128)(2,1)} %g_in.1) | copy-start | bytes 786436
  8.1 0.9 %copy-start.7 = (bf16[256,512]{1,0:T(8,128)(2,1)S(1)}, bf16[256,512]{1,0:T(8,128)(2,1)}, u32[]{:S(2)}) copy-start(bf16[256,512]{1,0:T(8,128)(2,1)} %o_in.1) | copy-start | bytes 786436

commit v2 on v1

--- a/solution.py
+++ b/solution.py
@@ -244,9 +244,9 @@
 def fused_kernel(outer, inner, n_dp, n_ctx, v_in, g_in, o_in, f_in, s_ref, fh_in, fl_in, ih_in, il_in,
                  mixed_out, ggate_out, gval_out, gfil_out,
                  v_ref, g_ref, o_ref, f_ref, fh, fl, ih, il, ahi, alo, spec, back,
-                 mixed_ref, ggate_ref, gval_ref, gfil_ref, rs_buf, piece,
+                 mixed_ref, ggate_ref, gval_ref, gfil_ref, x_buf, z_buf, sum_ref,
                  tab_sem, own_sem, in_send, in_recv, out_send, out_recv,
-                 rs_send, rs_recv, pc_send, pc_recv, bc_send, bc_recv):
+                 x_send, x_recv, z_send, z_recv, pc_send, pc_recv, ag_send, fw_send, ag_recv):
     half = outer // 2
     length, width = v_ref.shape
     rows_here = length // n_ctx
@@ -258,8 +258,12 @@
     def ctx_at(step):
         return lax.rem(ctx + step + n_ctx, n_ctx)
 
-    def dp_at(step):
-        return lax.rem(dp + step + n_dp, n_dp)
+    n_z = n_dp // 2
+    z, x = dp // 2, lax.rem(dp, 2)
+    across = 2 * z + 1 - x
+
+    def z_at(step):
+        return lax.rem(z + step + n_z, n_z)
 
     def block_rows(p):
         return pl.ds(pl.multiple_of(p * rows_here, 16), rows_here)
@@ -282,9 +286,10 @@
     barrier = pltpu.get_barrier_semaphore()
     for step in range(1, n_ctx):
         pl.semaphore_signal(barrier, inc=1, device_id={"context": ctx_at(step)}, device_id_type=MESH)
-    for step in range(1, n_dp):
-        pl.semaphore_signal(barrier, inc=1, device_id={"dp": dp_at(step)}, device_id_type=MESH)
-    pl.semaphore_wait(barrier, n_ctx - 1 + n_dp - 1)
+    pl.semaphore_signal(barrier, inc=1, device_id={"dp": across}, device_id_type=MESH)
+    for step in range(1, n_z):
+        pl.semaphore_signal(barrier, inc=1, device_id={"dp": 2 * z_at(step) + x}, device_id_type=MESH)
+    pl.semaphore_wait(barrier, n_ctx - 1 + 1 + n_z - 1)
 
     def inbound(i, step):
         src, dst = arrays[i]
@@ -308,7 +313,7 @@
             device_id_type=MESH,
         )
 
-    for i in range(4):
+    for i in range(3):
         for step in range(1, n_ctx):
             outbound_in(i, step).start()
 
@@ -357,6 +362,8 @@
     strips(spread_values)
     arrived(1)
     arrived(2)
+    for step in range(1, n_ctx):
+        outbound_in(3, step).start()
 
     def spread_grads(row):
         spread(1, [take(g_ref, a, row) * take(o_ref, a, row) for a in range(half)], row)
@@ -385,19 +392,31 @@
         place = lax.rem(d, n_ctx) * (n_dp // n_ctx) + d // n_ctx
         return pl.ds(pl.multiple_of(place * rows_piece, 8), rows_piece)
 
-    scatter = [
-        pltpu.make_async_remote_copy(
-            src_ref=gfil_ref.at[piece_rows(dp_at(step)), :],
-            dst_ref=rs_buf.at[step],
-            send_sem=rs_send.at[step],
-            recv_sem=rs_recv.at[step],
-            device_id={"dp": dp_at(step)},
+    cross = {
+        step: pltpu.make_async_remote_copy(
+            src_ref=gfil_ref.at[piece_rows(2 * z_at(step) + 1 - x), :],
+            dst_ref=x_buf.at[step],
+            send_sem=x_send.at[step],
+            recv_sem=x_recv.at[step],
+            device_id={"dp": across},
             device_id_type=MESH,
         )
-        for step in range(1, n_dp)
-    ]
-    for copy in scatter:
-        copy.start()
+        for step in range(n_z)
+    }
+    order = sorted(range(1, n_z), key=lambda step: abs(step - n_z // 2)) + [0]
+    for step in order:
+        cross[step].start()
+    along = {
+        step: pltpu.make_async_remote_copy(
+            src_ref=x_buf.at[step],
+            dst_ref=z_buf.at[step],
+            send_sem=z_send.at[step],
+            recv_sem=z_recv.at[step],
+            device_id={"dp": 2 * z_at(step) + x},
+            device_id_type=MESH,
+        )
+        for step in range(1, n_z)
+    }
 
     arrived(3)
 
@@ -416,7 +435,13 @@
         invert(k, 1, gr * fr + gi * fi, gi * fr - gr * fi)
         return carry
 
-    lax.fori_loop(0, half + 1, second, 0)
+    middle = (half + 1) // 2
+    lax.fori_loop(0, middle, second, 0)
+    for step in order[:-1]:
+        cross[step].wait_recv()
+        x_buf[step] = x_buf[step] + gfil_ref[piece_rows(2 * z_at(step) + x), :]
+        along[step].start()
+    lax.fori_loop(middle, half + 1, second, 0)
     skip = s_ref[...]
 
     def finish(row):
@@ -433,6 +458,50 @@
             gval_ref[rows(a), :] = (conv + skip * gm).astype(jnp.bfloat16)
 
     strips(finish)
+
+    cross[0].wait_recv()
+    total = gfil_ref[piece_rows(dp), :] + x_buf[0]
+    for step in range(1, n_z):
+        along[step].wait_recv()
+        total = total + z_buf[step]
+    sum_ref[...] = total
+
+    holder = lax.rem(dp, n_ctx)
+    part = dp // n_ctx
+    gap = lax.rem(ctx - holder + n_ctx, n_ctx)
+
+    def part_of(j, c):
+        return gfil_out.at[pl.ds(pl.multiple_of(j * rows_piece, 8), rows_piece), block_cols(c)]
+
+    def collect(which, c):
+        return pltpu.make_async_remote_copy(
+            src_ref=sum_ref,
+            dst_ref=part_of(part, c),
+            send_sem=pc_send.at[which],
+            recv_sem=pc_recv.at[which],
+            device_id={"context": holder},
+            device_id_type=MESH,
+        )
+
+    def relay(j, c, target, sem):
+        return pltpu.make_async_remote_copy(
+            src_ref=part_of(j, c),
+            dst_ref=part_of(j, c),
+            send_sem=sem,
+            recv_sem=ag_recv.at[j, c],
+            device_id={"dp": target},
+            device_id_type=MESH,
+        )
+
+    def onward(step, c):
+        return relay(part, c, 2 * z_at(step) + x, ag_send.at[step, c])
+
+    def sideways(j, c):
+        return relay(j, c, across, fw_send.at[j, c])
+
+    @pl.when(ctx != holder)
+    def _():
+        collect(gap, ctx).start()
 
     results = ((mixed_ref, mixed_out), (ggate_ref, ggate_out), (gval_ref, gval_out))
 
@@ -457,61 +526,54 @@
     for copy in kept:
         copy.start()
 
-    total = gfil_ref[piece_rows(dp), :]
-    for step, copy in zip(range(1, n_dp), scatter):
-        copy.wait_recv()
-        total = total + rs_buf[step]
-    piece[:, block_cols(ctx)] = total
-
-    holder = lax.rem(dp, n_ctx)
-    part = dp // n_ctx
-    gap = lax.rem(ctx - holder + n_ctx, n_ctx)
-
-    def part_rows(j):
-        return pl.ds(pl.multiple_of(j * rows_piece, 8), rows_piece)
-
-    def collect(which, c):
-        return pltpu.make_async_remote_copy(
-            src_ref=piece.at[:, block_cols(c)],
-            dst_ref=piece.at[:, block_cols(c)],
-            send_sem=pc_send.at[which],
-            recv_sem=pc_recv.at[which],
-            device_id={"context": holder},
-            device_id_type=MESH,
-        )
-
-    def cast(step, j):
-        return pltpu.make_async_remote_copy(
-            src_ref=piece,
-            dst_ref=gfil_out.at[part_rows(j), :],
-            send_sem=bc_send.at[step],
-            recv_sem=bc_recv.at[j],
-            device_id={"dp": dp_at(step)},
-            device_id_type=MESH,
-        )
+    @pl.when(ctx == holder)
+    def _():
+        mine = pltpu.make_async_copy(sum_ref, part_of(part, ctx), own_sem.at[3])
+        mine.start()
+        mine.wait()
+        for gap_here in range(n_ctx):
+            c = ctx_at(gap_here)
+            if gap_here:
+                collect(gap_here, c).wait_recv()
+            for step in order[:-1]:
+                onward(step, c).start()
+            sideways(part, c).start()
+
+    parts = n_dp // n_ctx
+    relays = []
+    for j in range(parts):
+        source = ctx + j * n_ctx
+        relays.append(jnp.logical_and(lax.rem(source, 2) == x, source != dp))
+
+    for gap_here in range(n_ctx):
+        for j in range(parts):
+            c = lax.rem(ctx + gap_here, n_ctx)
+
+            @pl.when(relays[j])
+            def _():
+                sideways(j, c).wait_recv()
+                sideways(j, c).start()
+
+    for j in range(parts):
+        @pl.when(lax.rem(ctx + j * n_ctx, 2) != x)
+        def _():
+            for c in range(n_ctx):
+                sideways(j, c).wait_recv()
+
+        @pl.when(lax.rem(ctx + j * n_ctx, 2) == x)
+        def _():
+            for c in range(n_ctx):
+                sideways(j, c).wait_send()
+
+    @pl.when(ctx == holder)
+    def _():
+        for gap_here in range(n_ctx):
+            for step in order[:-1]:
+                onward(step, ctx_at(gap_here)).wait_send()
 
     @pl.when(ctx != holder)
     def _():
-        copy = collect(gap, ctx)
-        copy.start()
-        copy.wait_send()
-
-    @pl.when(ctx == holder)
-    def _():
-        for step in range(1, n_ctx):
-            collect(step, ctx_at(step)).wait_recv()
-        for step in range(1, n_dp):
-            cast(step, part).start()
-        mine = pltpu.make_async_copy(piece, gfil_out.at[part_rows(part), :], own_sem.at[3])
-        mine.start()
-        mine.wait()
-        for step in range(1, n_dp):
-            cast(step, part).wait_send()
-
-    for j in range(n_dp // n_ctx):
-        @pl.when(dp != ctx + j * n_ctx)
-        def _():
-            cast(1, j).wait_recv()
+        collect(gap, ctx).wait_send()
 
     for copy in kept:
         copy.wait()
@@ -522,8 +584,26 @@
     for i in range(4):
         for step in range(1, n_ctx):
             outbound_in(i, step).wait_send()
-    for copy in scatter:
-        copy.wait_send()
+    for step in range(n_z):
+        cross[step].wait_send()
+    for step in range(1, n_z):
+        along[step].wait_send()
+
+
+def hand_over_kernel(*refs):
+    count = len(refs) // 2
+    for src, dst in zip(refs[:count], refs[count:]):
+        dst[...] = src[...]
+
+
+def hand_over(arrays):
+    vmem = pl.BlockSpec(memory_space=pltpu.VMEM)
+    return pl.pallas_call(
+        hand_over_kernel,
+        out_shape=[jax.ShapeDtypeStruct(x.shape, x.dtype) for x in arrays],
+        in_specs=[vmem] * len(arrays),
+        out_specs=[vmem] * len(arrays),
+    )(*arrays)
 
 
 def fused(values, gates, grads, filters, skips, n_dp, n_ctx):
@@ -553,13 +633,16 @@
         ]
         + [pltpu.VMEM(full, t) for t in (bf16, bf16, bf16, f32)]
         + [
-            pltpu.VMEM((n_dp, rows_piece, width), f32),
-            pltpu.VMEM((rows_piece, columns), f32),
+            pltpu.VMEM((n_dp // 2, rows_piece, width), f32),
+            pltpu.VMEM((n_dp // 2, rows_piece, width), f32),
+            pltpu.VMEM((rows_piece, width), f32),
             dma((4,)), dma((4,)), dma((4, n_ctx)), dma((4, n_ctx)), dma((3, n_ctx)), dma((3, n_ctx)),
-            dma((n_dp,)), dma((n_dp,)), dma((n_ctx,)), dma((n_ctx,)), dma((n_dp,)), dma((n_dp // n_ctx,)),
+            dma((n_dp // 2,)), dma((n_dp // 2,)), dma((n_dp // 2,)), dma((n_dp // 2,)),
+            dma((n_ctx,)), dma((n_ctx,)),
+            dma((n_dp // 2, n_ctx)), dma((n_dp // n_ctx, n_ctx)), dma((n_dp // n_ctx, n_ctx)),
         ],
         compiler_params=pltpu.CompilerParams(
-            collective_id=0, has_side_effects=True, vmem_limit_bytes=48 * 2**20
+            collective_id=0, has_side_effects=True, vmem_limit_bytes=60 * 2**20
         ),
     )(values, gates, grads, filters, skips, *(jnp.asarray(t) for t in tables(length)))
 
@@ -572,8 +655,8 @@
     to_rows = partial(lax.all_to_all, axis_name="context", split_axis=0, concat_axis=1, tiled=True)
     mine = lax.dynamic_slice_in_dim(skips, lax.axis_index("context") * width, width, 0)
     n_dp = lax.axis_size("dp")
-    if width % LANES == 0 and n_dp % group == 0:
-        return tuple(fused(values, gates, grad_out, filters, mine[None, :], n_dp, group))
+    if width % LANES == 0 and n_dp % group == 0 and n_dp % 2 == 0 and group % 2 == 0:
+        return tuple(hand_over(fused(values, gates, grad_out, filters, mine[None, :], n_dp, group)))
     mixed, ggate, gval, gfil = local_mix(
         to_channels(values), to_channels(gates), to_channels(grad_out), to_channels(filters), mine[None, :]
     )

time: 73.3 us -> 52.9 us (0.72); the launches traced: 72.1 us -> 52.7 us
  local copies, waits for them, and re-layouts: 11.4 us -> 1.26 us
  Pallas kernels: 60.1 us -> 50.8 us
    pallas_call x1, Pallas kernels: 60.1 us -> 48.4 us  [fused(): pl.pallas_call(partial(fused_kernel, outer, inner, n_dp, n_ctx), out_shap...]
    unnamed x20 -> x2, local copies, waits for them, and re-layouts: 11.3 us -> 0.68 us
    pallas_call x0 -> x1, Pallas kernels: none -> 2.35 us  [hand_over(): pl.pallas_call(hand_over_kernel, out_shape=[jax.ShapeDtypeStruct(x.shape,...]
where the time goes in v2:
time: 52.9 us; the launch traced here: 52.7 us
  Pallas kernels  50.8 us (96%)
  local copies, waits for them, and re-layouts  1.26 us (2%)
  between operations  0.65 us (1%)
    pallas_call x1, Pallas kernels, fused(): pl.pallas_call(partial(fused_kernel, outer, inner, n_dp, n_ctx), out_shap...  48.4 us
    pallas_call x1, Pallas kernels, hand_over(): pl.pallas_call(hand_over_kernel, out_shape=[jax.ShapeDtypeStruct(x.shape,...  2.35 us

profile of v2, /device:TPU:26, one launch (start us, length us, event | category | flops | bytes accessed | tf_op | source)
XLA Modules:
  0.0 52.7 jit_solution(9922958360775917591)
XLA Ops:
  0.6 0.0 copy-start
  0.6 0.7 %copy-done = f32[512]{0:T(512)S(1)} copy-done((f32[512]{0:T(512)S(1)}, f32[512]{0:T(512)}, u32[]{:S(2)}) %copy-start) | copy-done | bytes 2072
  1.3 0.6 %dynamic-slice_bitcast_fusion.s_ref = f32[1,128]{1,0:T(1,128)} fusion(f32[512]{0:T(512)S(1)} %copy-done, s32[]{:T(128)S(6)} %select_n.3), kind=kLoop, calls=%fused_computation | loop fusion | bytes 1028 | tf_op jit(solution)/shard_map/broadcast_in_dim | solution.py:659
  1.9 48.4 %shard_map.120 = (bf16[256,512]{1,0:T(8,128)(2,1)}, bf16[256,512]{1,0:T(8,128)(2,1)}, bf16[256,512]{1,0:T(8,128)(2,1)}, f32[256,512]{1,0:T(8,128)}) custom-call(bf16[256,512]{1,0:T(8,128)(2,1)} %v_in.1, bf16[256,512]{1,0:T(8,128)(2,1)} %g_in.1, bf16[256,512]{1,0:T(8,128)(2,1)} %o_in.1, f32[256,512]{1,0:T(8,128)} %f_in.1, ...), custom_call_target="tpu_custom_call" | custom-call | tf_op jit(solution)/shard_map/pallas_call | solution.py:621
  50.3 2.4 %shard_map.121 = (bf16[256,512]{1,0:T(8,128)(2,1)}, bf16[256,512]{1,0:T(8,128)(2,1)}, bf16[256,512]{1,0:T(8,128)(2,1)}, f32[256,512]{1,0:T(8,128)}) custom-call(bf16[256,512]{1,0:T(8,128)(2,1)} %get-tuple-element.8.refs_0_, bf16[256,512]{1,0:T(8,128)(2,1)} %get-tuple-element.9.refs_1_, bf16[256,512]{1,0:T(8,128)(2,1)} %get-tuple-element.10.refs_2_, ...), custom_call_target="tpu_custom_call" | custom-call | tf_op jit(solution)/shard_map/pallas_call | solution.py:601
Async XLA Ops:
  0.6 0.7 %copy-start = (f32[512]{0:T(512)S(1)}, f32[512]{0:T(512)}, u32[]{:S(2)}) copy-start(f32[512]{0:T(512)} %param.12) | copy-start | bytes 6148

commit v3 on v2

--- a/solution.py
+++ b/solution.py
@@ -457,7 +457,6 @@
             gm = take(g_ref, a, row) * take(o_ref, a, row)
             gval_ref[rows(a), :] = (conv + skip * gm).astype(jnp.bfloat16)
 
-    strips(finish)
 
     cross[0].wait_recv()
     total = gfil_ref[piece_rows(dp), :] + x_buf[0]
@@ -503,6 +502,7 @@
     def _():
         collect(gap, ctx).start()
 
+    strips(finish)
     results = ((mixed_ref, mixed_out), (ggate_ref, ggate_out), (gval_ref, gval_out))
 
     def returned(i, step, landing):

time: 52.9 us -> 53.6 us (1.013)
  Pallas kernels: 50.8 us -> 51.5 us
    pallas_call x1, Pallas kernels: 48.4 us -> 49.1 us  [fused(): pl.pallas_call(partial(fused_kernel, outer, inner, n_dp, n_ctx), out_shap...]
where the time goes in v3:
time: 53.6 us; the launch traced here: 53.4 us
  Pallas kernels  51.5 us (96%)
  local copies, waits for them, and re-layouts  1.26 us (2%)
  between operations  0.65 us (1%)
    pallas_call x1, Pallas kernels, fused(): pl.pallas_call(partial(fused_kernel, outer, inner, n_dp, n_ctx), out_shap...  49.1 us
    pallas_call x1, Pallas kernels, hand_over(): pl.pallas_call(hand_over_kernel, out_shape=[jax.ShapeDtypeStruct(x.shape,...  2.35 us

profile of v3, /device:TPU:26, one launch (start us, length us, event | category | flops | bytes accessed | tf_op | source)
XLA Modules:
  0.0 53.4 jit_solution(5284246035303409754)
XLA Ops:
  0.6 0.0 copy-start
  0.6 0.7 %copy-done = f32[512]{0:T(512)S(1)} copy-done((f32[512]{0:T(512)S(1)}, f32[512]{0:T(512)}, u32[]{:S(2)}) %copy-start) | copy-done | bytes 2072
  1.3 0.6 %dynamic-slice_bitcast_fusion.s_ref = f32[1,128]{1,0:T(1,128)} fusion(f32[512]{0:T(512)S(1)} %copy-done, s32[]{:T(128)S(6)} %select_n.3), kind=kLoop, calls=%fused_computation | loop fusion | bytes 1028 | tf_op jit(solution)/shard_map/broadcast_in_dim | solution.py:659
  1.9 49.1 %shard_map.120 = (bf16[256,512]{1,0:T(8,128)(2,1)}, bf16[256,512]{1,0:T(8,128)(2,1)}, bf16[256,512]{1,0:T(8,128)(2,1)}, f32[256,512]{1,0:T(8,128)}) custom-call(bf16[256,512]{1,0:T(8,128)(2,1)} %v_in.1, bf16[256,512]{1,0:T(8,128)(2,1)} %g_in.1, bf16[256,512]{1,0:T(8,128)(2,1)} %o_in.1, f32[256,512]{1,0:T(8,128)} %f_in.1, ...), custom_call_target="tpu_custom_call" | custom-call | tf_op jit(solution)/shard_map/pallas_call | solution.py:621
  51.1 2.4 %shard_map.121 = (bf16[256,512]{1,0:T(8,128)(2,1)}, bf16[256,512]{1,0:T(8,128)(2,1)}, bf16[256,512]{1,0:T(8,128)(2,1)}, f32[256,512]{1,0:T(8,128)}) custom-call(bf16[256,512]{1,0:T(8,128)(2,1)} %get-tuple-element.8.refs_0_, bf16[256,512]{1,0:T(8,128)(2,1)} %get-tuple-element.9.refs_1_, bf16[256,512]{1,0:T(8,128)(2,1)} %get-tuple-element.10.refs_2_, ...), custom_call_target="tpu_custom_call" | custom-call | tf_op jit(solution)/shard_map/pallas_call | solution.py:601
Async XLA Ops:
  0.6 0.7 %copy-start = (f32[512]{0:T(512)S(1)}, f32[512]{0:T(512)}, u32[]{:S(2)}) copy-start(f32[512]{0:T(512)} %param.12) | copy-start | bytes 6148
